TPU v7x, 32 devices: a whole 2x2x4 slice. The times are simulated.
32 devices in a mesh: dp: 8 (over z, core), tensor: 4 (over y, x).
Axes of the slice: x: 2, y: 2, z: 4, core: 2. Of those that a mesh axis runs over, the one named last changes fastest.
Arguments:
- hidden: bfloat16 [6144, 2048], P('dp'), may hold values from -6 to 6
- kv_input: bfloat16 [6144, 2048], P('dp'), may hold values from -6 to 6
- attn_norm: float32 [2048], replicated, may hold values from 0.1 to 1.9
- w_query: bfloat16 [2048, 2048], P(None, 'tensor'), may hold values from -0.125 to 0.125
- w_key: bfloat16 [2048, 2048], P(None, 'tensor'), may hold values from -0.125 to 0.125
- w_value: bfloat16 [2048, 2048], P(None, 'tensor'), may hold values from -0.125 to 0.125
- w_out: bfloat16 [2048, 2048], P('tensor'), may hold values from -1 to 1
- kv_norm: float32 [2048], replicated, may hold values from 0.1 to 1.9
- ffn_norm: float32 [2048], replicated, may hold values from 0.1 to 1.9
- w_gate: bfloat16 [2048, 5504], P(None, 'tensor'), may hold values from -0.125 to 0.125
- w_up: bfloat16 [2048, 5504], P(None, 'tensor'), may hold values from -0.125 to 0.125
- w_down: bfloat16 [5504, 2048], P('tensor'), may hold values from -0.078125 to 0.078125
- seq_lengths: int32 [8, 2], P('dp'), may hold values from 0 to 768, as said below
- cotangent: bfloat16 [6144, 2048], P('dp'), may hold values from -6 to 6
Outputs:
- output: bfloat16 [6144, 2048], P('dp')
- grad_input: bfloat16 [6144, 2048], P('dp')
- grad_kv_input: bfloat16 [6144, 2048], P('dp')
- grad_attn_norm: float32 [2048], P('dp')
- grad_query: float32 [2048, 2048], P('dp', 'tensor')
- grad_key: float32 [2048, 2048], P('dp', 'tensor')
- grad_value: float32 [2048, 2048], P('dp', 'tensor')
- grad_out: float32 [2048, 2048], P('tensor', 'dp')
- grad_kv_norm: float32 [2048], P('dp')
- grad_ffn_norm: float32 [2048], P('dp')
- grad_gate: float32 [2048, 5504], P('dp', 'tensor')
- grad_up: float32 [2048, 5504], P('dp', 'tensor')
- grad_down: float32 [5504, 2048], P('tensor', 'dp')
Inputs may be any that keep to these rules, and one draw needn't show every extreme that they name: `seq_lengths`: in each row the two lengths sum to 384 or more and to 768 at most, and the first is at least half of that sum, rounded down; in every draw one row holds a single sequence of exactly 768 tokens and a second length 0.
All inputs are finite; a program needn't handle non-finite values.
Results may differ from a plain program's by a relative error of at most 0.015.
Values sent between devices are 32-bit elements; how exact they have to be, the bound alone decides.
A program may use at most 256 MiB of HBM per device.

v0:
```python
import jax
import jax.numpy as jnp
from jax import lax
from jax.sharding import PartitionSpec as P

HEAD_DIM = 128


def norm_scale(values):
    return lax.rsqrt(jnp.mean(values * values, axis=-1, keepdims=True) + 1e-06)


def left_dot(left, right):
    return lax.dot_general(
        left, right, (((0,), (0,)), ((), ())), preferred_element_type=jnp.float32
    )


def right_dot(left, right):
    return lax.dot_general(
        left, right, (((1,), (1,)), ((), ())), preferred_element_type=jnp.float32
    )


def norm_back(d_normed, unit, scale_row, gain):
    gain_grad = jnp.sum(d_normed * unit, axis=0)
    d_unit = d_normed * gain
    d_in = scale_row * (d_unit - unit * jnp.mean(d_unit * unit, axis=-1, keepdims=True))
    return (gain_grad, d_in)


def body(
    hidden,
    kv_input,
    attn_norm,
    w_query,
    w_key,
    w_value,
    w_out,
    kv_norm,
    ffn_norm,
    w_gate,
    w_up,
    w_down,
    seq_lengths,
    cotangent,
):
    rows = hidden.shape[0]
    width = w_query.shape[1]
    heads = width // HEAD_DIM
    scale = HEAD_DIM ** (-0.5)
    first = seq_lengths[0, 0]
    total = first + seq_lengths[0, 1]
    places = jnp.arange(rows, dtype=jnp.int32)
    segment = (places >= first).astype(jnp.int32) + (places >= total).astype(jnp.int32)
    allowed = (segment[:, None] == segment[None, :]) & (places[None, :] <= places[:, None])
    live = (places < total).astype(jnp.float32)[:, None]
    x_full = hidden.astype(jnp.float32)
    scale_attn = norm_scale(x_full)
    unit_attn = x_full * scale_attn
    normed = (unit_attn * attn_norm).astype(jnp.bfloat16)
    query = jnp.dot(normed, w_query, preferred_element_type=jnp.float32).astype(jnp.bfloat16)
    kv_full = kv_input.astype(jnp.float32)
    scale_kv = norm_scale(kv_full)
    unit_kv = kv_full * scale_kv
    kv_normed = (unit_kv * kv_norm).astype(jnp.bfloat16)
    keys = jnp.dot(kv_normed, w_key, preferred_element_type=jnp.float32).astype(jnp.bfloat16)
    values = jnp.dot(kv_normed, w_value, preferred_element_type=jnp.float32).astype(jnp.bfloat16)
    q_heads = query.reshape(rows, heads, HEAD_DIM)
    k_heads = keys.reshape(rows, heads, HEAD_DIM)
    v_heads = values.reshape(rows, heads, HEAD_DIM)

    def scores_of():
        raw = (
            jnp.einsum("qhd,khd->hqk", q_heads, k_heads, preferred_element_type=jnp.float32) * scale
        )
        return jnp.where(allowed[None], raw, -1e30)

    scores = scores_of()
    peak = jnp.max(scores, axis=-1, keepdims=True)
    weights = jnp.exp(scores - peak)
    row_total = jnp.sum(weights, axis=-1, keepdims=True)
    log_total = peak + jnp.log(row_total)
    probs_low = (weights / row_total).astype(jnp.bfloat16)
    attended = jnp.einsum("hqk,khd->qhd", probs_low, v_heads, preferred_element_type=jnp.float32)
    attended = attended.astype(jnp.bfloat16).reshape(rows, width)
    branch = lax.psum(jnp.dot(attended, w_out, preferred_element_type=jnp.float32), "tensor")
    resid = x_full + branch
    scale_ffn = norm_scale(resid)
    unit_ffn = resid * scale_ffn
    ffn_in = (unit_ffn * ffn_norm).astype(jnp.bfloat16)
    gate_pre, up_pre = (
        jnp.dot(ffn_in, w_gate, preferred_element_type=jnp.float32),
        jnp.dot(ffn_in, w_up, preferred_element_type=jnp.float32),
    )
    activated = (jax.nn.silu(gate_pre) * up_pre).astype(jnp.bfloat16)
    ffn_out = lax.psum(jnp.dot(activated, w_down, preferred_element_type=jnp.float32), "tensor")
    output = ((resid + ffn_out) * live).astype(jnp.bfloat16)
    d_out = cotangent.astype(jnp.float32) * live
    d_out_low = d_out.astype(jnp.bfloat16)
    grad_down = left_dot(activated, d_out_low)
    d_act = right_dot(d_out_low, w_down)
    gate_use, up_use = (gate_pre, up_pre)
    sigma = jax.nn.sigmoid(gate_use)
    d_gate = (d_act * up_use * sigma * (1.0 + gate_use * (1.0 - sigma))).astype(jnp.bfloat16)
    d_up = (d_act * gate_use * sigma).astype(jnp.bfloat16)
    grad_gate = left_dot(ffn_in, d_gate)
    grad_up = left_dot(ffn_in, d_up)
    d_ffn_in = lax.psum(right_dot(d_gate, w_gate) + right_dot(d_up, w_up), "tensor")
    grad_ffn_norm, d_res_norm = norm_back(d_ffn_in, unit_ffn, scale_ffn, ffn_norm)
    d_resid = d_out + d_res_norm
    d_branch = d_resid.astype(jnp.bfloat16)
    grad_out = left_dot(attended, d_branch)
    d_att = right_dot(d_branch, w_out).astype(jnp.bfloat16).reshape(rows, heads, HEAD_DIM)
    probs = jnp.exp(scores_of() - log_total)
    probs_back = probs.astype(jnp.bfloat16)
    d_probs = jnp.einsum("qhd,khd->hqk", d_att, v_heads, preferred_element_type=jnp.float32)
    d_values = jnp.einsum("hqk,qhd->khd", probs_back, d_att, preferred_element_type=jnp.float32)
    d_values = d_values.astype(jnp.bfloat16).reshape(rows, width)
    inner = jnp.sum(probs * d_probs, axis=-1, keepdims=True)
    d_scores = (probs * (d_probs - inner)).astype(jnp.bfloat16)
    d_query = (
        jnp.einsum("hqk,khd->qhd", d_scores, k_heads, preferred_element_type=jnp.float32) * scale
    )
    d_query = d_query.astype(jnp.bfloat16).reshape(rows, width)
    d_keys = (
        jnp.einsum("hqk,qhd->khd", d_scores, q_heads, preferred_element_type=jnp.float32) * scale
    )
    d_keys = d_keys.astype(jnp.bfloat16).reshape(rows, width)
    grad_query = left_dot(normed, d_query)
    grad_key = left_dot(kv_normed, d_keys)
    grad_value = left_dot(kv_normed, d_values)
    d_normed, d_kv_normed = lax.psum(
        (right_dot(d_query, w_query), right_dot(d_keys, w_key) + right_dot(d_values, w_value)),
        "tensor",
    )
    grad_attn_norm, d_x = norm_back(d_normed, unit_attn, scale_attn, attn_norm)
    grad_kv_norm, d_kv = norm_back(d_kv_normed, unit_kv, scale_kv, kv_norm)
    grad_input = (d_resid + d_x).astype(jnp.bfloat16)
    grad_kv_input = d_kv.astype(jnp.bfloat16)
    parts = (
        lax.psum_scatter(grad_attn_norm, "dp", scatter_dimension=0, tiled=True),
        lax.psum_scatter(grad_query, "dp", scatter_dimension=0, tiled=True),
        lax.psum_scatter(grad_key, "dp", scatter_dimension=0, tiled=True),
        lax.psum_scatter(grad_value, "dp", scatter_dimension=0, tiled=True),
        lax.psum_scatter(grad_out, "dp", scatter_dimension=1, tiled=True),
        lax.psum_scatter(grad_kv_norm, "dp", scatter_dimension=0, tiled=True),
        lax.psum_scatter(grad_ffn_norm, "dp", scatter_dimension=0, tiled=True),
        lax.psum_scatter(grad_gate, "dp", scatter_dimension=0, tiled=True),
        lax.psum_scatter(grad_up, "dp", scatter_dimension=0, tiled=True),
        lax.psum_scatter(grad_down, "dp", scatter_dimension=1, tiled=True),
    )
    return (
        output,
        grad_input,
        grad_kv_input,
        parts[0],
        parts[1],
        parts[2],
        parts[3],
        parts[4],
        parts[5],
        parts[6],
        parts[7],
        parts[8],
        parts[9],
    )


def solution(mesh):
    in_specs = (
        P("dp", None),
        P("dp", None),
        P(),
        P(None, "tensor"),
        P(None, "tensor"),
        P(None, "tensor"),
        P("tensor", None),
        P(),
        P(),
        P(None, "tensor"),
        P(None, "tensor"),
        P("tensor", None),
        P("dp", None),
        P("dp", None),
    )
    out_specs = (
        P("dp", None),
        P("dp", None),
        P("dp", None),
        P("dp"),
        P("dp", "tensor"),
        P("dp", "tensor"),
        P("dp", "tensor"),
        P("tensor", "dp"),
        P("dp"),
        P("dp"),
        P("dp", "tensor"),
        P("dp", "tensor"),
        P("tensor", "dp"),
    )
    return jax.shard_map(body, mesh=mesh, in_specs=in_specs, out_specs=out_specs, check_vma=False)
```

profile of v0, /device:TPU:0, one launch (start us, length us, event | category | flops | bytes accessed | tf_op | source)
XLA Modules:
  0.0 1327.6 jit_solution(16951520881639728668)
XLA Ops:
  7.2 1.4 fusion.56
  10.0 0.8 convert_add_fusion.1
  10.8 3.0 fusion.24
  13.8 2.6 fusion.16
  16.8 2.0 convolution_convert_fusion
  18.9 2.0 convolution_convert_fusion.2
  20.9 0.5 copy-done.24
  21.4 2.0 convolution_convert_fusion.1
  23.4 1.9 fusion.57
  25.3 1.3 fusion.4
  26.6 2.1 fusion.38
  29.0 0.9 copy-done.19
  29.9 4.5 fusion.58
  34.5 141.2 %all-reduce.9.cloned.1.call-done = f32[768,2048]{1,0:T(8,128)} async-done(((f32[768,2048]{1,0:T(8,128)}), f32[768,2048]{1,0:T(8,128)}) %all-reduce.9.cloned.1.call-update) | async-done | bytes 6291472 | tf_op jit(solution)/shard_map/psum | solution.py:87
  175.7 4.6 multiply_reduce_fusion.3
  180.3 0.6 multiply_convert_fusion.2
  181.0 12.8 fusion.60
  193.8 6.5 fusion.59
  200.3 11.8 multiply_convert_fusion.3
  212.1 7.5 fusion.62
  219.7 7.3 convolution_add_fusion.1
  227.0 9.8 fusion.61
  236.9 128.7 %all-reduce.11.cloned.1.call-done = f32[768,2048]{1,0:T(8,128)} async-done(((f32[768,2048]{1,0:T(8,128)}), f32[768,2048]{1,0:T(8,128)}) %all-reduce.11.cloned.1.call-update) | async-done | bytes 6291472 | tf_op jit(solution)/shard_map/psum | solution.py:109
  365.6 5.6 multiply_reduce_fusion.1
  371.2 0.8 copy-done.11
  372.0 0.9 copy-done.18
  372.9 4.7 multiply_add_fusion
  377.7 1.9 fusion.35
  379.5 0.7 copy-done.5
  380.2 1.7 fusion.39
  382.0 4.8 multiply_reduce_fusion
  386.9 10.3 multiply_convert_fusion
  397.2 4.1 multiply_convert_fusion.6
  401.4 0.8 multiply_convert_fusion.7
  402.2 1.1 copy-done.25
  403.2 4.5 fusion.63
  407.7 1.8 fusion.64
  409.6 4.6 convolution_add_fusion
  414.2 1.1 copy-done.20
  415.3 6.6 fusion.31
  422.2 6.0 fusion.50
  428.2 6.4 fusion.52
  434.7 6.0 fusion.46
  440.7 11.4 fusion.42
  452.4 11.6 fusion.66
  464.1 11.7 fusion.65
  475.8 0.6 copy-done.33
  476.5 0.6 dynamic-slice
  477.7 280.2 %all-reduce.13.cloned.1.call-done = (f32[768,2048]{1,0:T(8,128)}, f32[768,2048]{1,0:T(8,128)}, f32[768,2048]{1,0:T(8,128)}) async-done(((f32[768,2048]{1,0:T(8,128)}, f32[768,2048]{1,0:T(8,128)}, f32[768,2048]{1,0:T(8,128)}), (f32[768,2048]{1,0:T(8,128)}, f32[768,2048]{1,0:T(8,128)}, f32[768,2048]{1,0:T(8,128)})) %all-reduce.13.cloned.1.call-update) | async-done | bytes 18874384 | tf_op jit(solution)/shard_map/psum | solution.py:97
  757.9 4.8 fusion.23
  762.7 0.7 copy-done.10
  763.4 3.5 fusion.15
  766.9 30.7 %all-reduce.3 = (f32[2048]{0:T(1024)S(1)}, f32[2048]{0:T(1024)S(1)}, f32[2048]{0:T(1024)S(1)}) all-reduce(f32[2048]{0:T(1024)S(1)} %get-tuple-element.17, f32[2048]{0:T(1024)S(1)} %get-tuple-element.15, f32[2048]{0:T(1024)S(1)} %get-tuple-element.13), channel_id=2, replica_groups=mesh['dp'=8,'tensor'=4] {'dp'}, use_global_device_ids=true, to_apply=%region_15.16.clone | all-reduce | flops 6144 | bytes 49152
  797.6 0.6 dynamic-slice.1
  798.2 0.6 dynamic-slice.3
  798.8 0.6 dynamic-slice.5
  799.5 7.1 multiply_convert_fusion.1
  806.7 10.4 fusion.14
  817.1 46.7 %reduce-scatter.12.cloned.1.call-done = f32[256,512]{1,0:T(8,128)} async-done(((f32[2048,512]{1,0:T(8,128)}), f32[256,512]{1,0:T(8,128)}) %reduce-scatter.12.cloned.1.call-update) | async-done | bytes 524304 | tf_op jit(solution)/shard_map/reduce_scatter | solution.py:145
  863.7 51.0 %reduce-scatter.10.cloned.1.call-done = f32[256,512]{1,0:T(8,128)} async-done(((f32[2048,512]{1,0:T(8,128)}), f32[256,512]{1,0:T(8,128)}) %reduce-scatter.10.cloned.1.call-update) | async-done | bytes 524304 | tf_op jit(solution)/shard_map/reduce_scatter | solution.py:144
  914.8 51.2 %reduce-scatter.8.cloned.1.call-done = f32[256,512]{1,0:T(8,128)} async-done(((f32[2048,512]{1,0:T(8,128)}), f32[256,512]{1,0:T(8,128)}) %reduce-scatter.8.cloned.1.call-update) | async-done | bytes 524304 | tf_op jit(solution)/shard_map/reduce_scatter | solution.py:143
  965.9 118.0 %reduce-scatter.20.cloned.1.call-done = f32[1376,256]{1,0:T(8,128)} async-done(((f32[1376,2048]{1,0:T(8,128)}), f32[1376,256]{1,0:T(8,128)}) %reduce-scatter.20.cloned.1.call-update) | async-done | bytes 1409040 | tf_op jit(solution)/shard_map/reduce_scatter | solution.py:151
  1083.9 118.2 %reduce-scatter.18.cloned.1.call-done = f32[256,1376]{0,1:T(8,128)} async-done(((f32[2048,1376]{0,1:T(8,128)}), f32[256,1376]{0,1:T(8,128)}) %reduce-scatter.18.cloned.1.call-update) | async-done | bytes 1409040 | tf_op jit(solution)/shard_map/reduce_scatter | solution.py:150
  1202.2 118.1 %reduce-scatter.16.cloned.1.call-done = f32[256,1376]{0,1:T(8,128)} async-done(((f32[2048,1376]{0,1:T(8,128)}), f32[256,1376]{0,1:T(8,128)}) %reduce-scatter.16.cloned.1.call-update) | async-done | bytes 1409040 | tf_op jit(solution)/shard_map/reduce_scatter | solution.py:149
  (106 shorter events, 2.0 us)
Async XLA Ops:
  7.2 22.7 %copy-start = (bf16[512,2048]{1,0:T(8,128)(2,1)S(1)}, bf16[512,2048]{1,0:T(8,128)(2,1)}, u32[]{:S(2)}) copy-start(bf16[512,2048]{1,0:T(8,128)(2,1)} %param.20) | copy-start | bytes 6291460
  7.2 9.5 copy-start.31
  7.2 168.5 %all-reduce.9.cloned.1.call-start = ((), (), s32[]{:S(2)}) async-start(), calls=%async_computation.7 | async-start | bytes 12582912 | tf_op jit(solution)/shard_map/psum | solution.py:87
  9.9 6.8 copy-start.8
  10.0 6.8 copy-start.26
  16.8 2.0 copy-start.22
  18.8 2.1 copy-start.6
  18.8 2.5 copy-start.24
  18.8 2.5 copy-start.32
  21.4 5.2 copy-start.28
  23.4 1.9 copy-start.13
  25.3 3.7 copy-start.2
  29.0 0.9 copy-start.19
  34.4 331.2 %all-reduce.11.cloned.1.call-start = ((), (), s32[]{:S(2)}) async-start(), calls=%async_computation.8 | async-start | bytes 12582912 | tf_op jit(solution)/shard_map/psum | solution.py:109
  34.4 145.9 %copy-start.30 = (f32[2048]{0:T(1024)S(1)}, f32[2048]{0:T(1024)}, u32[]{:S(2)}) copy-start(f32[2048]{0:T(1024)} %param.22) | copy-start | bytes 24580
  180.3 13.5 %copy-start.3 = (f32[768,2048]{1,0:T(8,128)}, f32[768,2048]{1,0:T(8,128)S(1)}, u32[]{:S(2)}) copy-start(f32[768,2048]{1,0:T(8,128)S(1)} %get-tuple-element.26) | copy-start | bytes 18874372
  180.3 13.5 %slice-start.5 = ((s8[5636096]{0:T(1024)(128)(4,1)}), s8[4194304]{0:T(1024)(128)(4,1)S(1)}, s32[]{:S(2)}) async-start(s8[5636096]{0:T(1024)(128)(4,1)} %bitcast.81), calls=%async_computation.22 | async-start | bytes 8388608
  180.9 12.8 copy-start.12
  180.9 12.8 slice-start.6
  193.8 6.5 copy-start.17
  193.8 25.9 %slice-start.3 = ((s8[5636096]{0:T(1024)(128)(4,1)}), s8[1441792]{0:T(1024)(128)(4,1)S(1)}, s32[]{:S(2)}) async-start(s8[5636096]{0:T(1024)(128)(4,1)} %bitcast.63), calls=%async_computation.20 | async-start | bytes 2883584
  200.3 19.3 %slice-start.4 = ((s8[5636096]{0:T(1024)(128)(4,1)}), s8[4194304]{0:T(1024)(128)(4,1)S(1)}, s32[]{:S(2)}) async-start(s8[5636096]{0:T(1024)(128)(4,1)} %bitcast.63), calls=%async_computation.21 | async-start | bytes 8388608
  212.1 7.5 copy-start.21
  227.0 530.9 %all-reduce.13.cloned.1.call-start = ((), (), s32[]{:S(2)}) async-start(), calls=%async_computation.16 | async-start | bytes 37748736 | tf_op jit(solution)/shard_map/psum | solution.py:97
  365.6 6.4 copy-start.11
  365.6 7.3 copy-start.18
  372.9 7.3 slice-start
  372.9 7.3 slice-start.1
  377.6 2.6 copy-start.5
  377.6 2.6 slice-start.2
  380.2 1.8 copy-start.29
  386.8 10.3 copy-start.14
  397.2 4.1 copy-start.4
  401.3 6.4 copy-start.15
  401.3 1.9 copy-start.25
  402.2 5.5 copy-start.27
  407.7 1.9 copy-start.23
  414.2 1.1 copy-start.20
  414.2 402.9 %reduce-scatter.14.cloned.1.call-start = ((), (), s32[]{:S(2)}) async-start(), calls=%async_computation.12 | async-start | bytes 4718592 | tf_op jit(solution)/shard_map/reduce_scatter | solution.py:146
  421.9 6.4 copy-start.16
  421.9 441.8 %reduce-scatter.12.cloned.1.call-start = ((), (), s32[]{:S(2)}) async-start(), calls=%async_computation.11 | async-start | bytes 4718592 | tf_op jit(solution)/shard_map/reduce_scatter | solution.py:145
  428.2 486.6 %reduce-scatter.10.cloned.1.call-start = ((), (), s32[]{:S(2)}) async-start(), calls=%async_computation.10 | async-start | bytes 4718592 | tf_op jit(solution)/shard_map/reduce_scatter | solution.py:144
  434.6 531.3 %reduce-scatter.8.cloned.1.call-start = ((), (), s32[]{:S(2)}) async-start(), calls=%async_computation.9 | async-start | bytes 4718592 | tf_op jit(solution)/shard_map/reduce_scatter | solution.py:143
  440.7 643.3 %reduce-scatter.20.cloned.1.call-start = ((), (), s32[]{:S(2)}) async-start(), calls=%async_computation.15 | async-start | bytes 12681216 | tf_op jit(solution)/shard_map/reduce_scatter | solution.py:151
  452.1 750.1 %reduce-scatter.18.cloned.1.call-start = ((), (), s32[]{:S(2)}) async-start(), calls=%async_computation.14 | async-start | bytes 12681216 | tf_op jit(solution)/shard_map/reduce_scatter | solution.py:150
  464.0 856.2 %reduce-scatter.16.cloned.1.call-start = ((), (), s32[]{:S(2)}) async-start(), calls=%async_computation.13 | async-start | bytes 12681216 | tf_op jit(solution)/shard_map/reduce_scatter | solution.py:149
  475.8 0.7 copy-start.33
  757.9 5.5 copy-start.10
  799.5 7.2 copy-start.7
  799.5 7.2 copy-start.9
  806.6 513.6 %copy-start.1 = (bf16[512,2048]{1,0:T(8,128)(2,1)S(1)}, bf16[512,2048]{1,0:T(8,128)(2,1)}, u32[]{:S(2)}) copy-start(bf16[512,2048]{1,0:T(8,128)(2,1)} %param.20) | copy-start | bytes 6291460
Sparse Core Ops, SparseCore 0:
  34.5 141.1 all-reduce.8
  227.1 138.4 all-reduce.10
  414.3 343.5 all-reduce.12
  760.7 51.9 reduce-scatter.13
  815.5 48.1 reduce-scatter.11
  866.5 48.1 reduce-scatter.9
  917.7 48.1 reduce-scatter.7
  968.9 114.9 reduce-scatter.19
  1086.9 115.1 reduce-scatter.17
  1205.0 115.1 reduce-scatter.15
where the time goes:
time: 1340 us; the launch traced here: 1330 us
  waiting for transfers between devices  1050 us (78%)
  matrix products  154 us (11%)
  other arithmetic  59.7 us (4%)
  blocking collectives  30.7 us (2%)
  between operations  17.2 us (1%)
    psum x1, waiting for transfers between devices, body(): lax.psum(jnp.dot(activated, w_down, preferred_element_type=jnp.float32),...  280 us
    psum x1, waiting for transfers between devices, body(): lax.psum(jnp.dot(attended, w_out, preferred_element_type=jnp.float32), 't...  141 us
    psum x1, waiting for transfers between devices, body(): lax.psum(right_dot(d_gate, w_gate) + right_dot(d_up, w_up), 'tensor')  129 us
    reduce_scatter x1, waiting for transfers between devices, body(): lax.psum_scatter(grad_up, 'dp', scatter_dimension=0, tiled=True)  118 us
    reduce_scatter x1, waiting for transfers between devices, body(): lax.psum_scatter(grad_gate, 'dp', scatter_dimension=0, tiled=True)  118 us
    reduce_scatter x1, waiting for transfers between devices, body(): lax.psum_scatter(grad_down, 'dp', scatter_dimension=1, tiled=True)  118 us
    dot_general x7, matrix products, left_dot(): lax.dot_general(left, right, (((0,), (0,)), ((), ())), preferred_element_...  59.6 us
    reduce_scatter x1, waiting for transfers between devices, body(): lax.psum_scatter(grad_query, 'dp', scatter_dimension=0, tiled=True)  51.2 us
  transfers between devices with their start and end apart: 10, of which 9 were waited for; matrix products, arithmetic and copies ran while one was open for 7% of the time, Pallas kernels for 0%

commit v1 on v0

v1 whole, which is shorter than its diff:
```python
import functools

import jax
import jax.numpy as jnp
from jax import lax
from jax.experimental import pallas as pl
from jax.experimental.pallas import tpu as pltpu
from jax.sharding import PartitionSpec as P

HEAD_DIM = 128
EPS = 1e-06
MESH = pl.DeviceIdType.MESH
ANY = pl.BlockSpec(memory_space=pl.ANY)
F32 = jnp.float32
BF16 = jnp.bfloat16


def norm_scale(values):
    return lax.rsqrt(jnp.mean(values * values, axis=-1, keepdims=True) + EPS)


def left_dot(left, right):
    return lax.dot_general(left, right, (((0,), (0,)), ((), ())), preferred_element_type=F32)


def right_dot(left, right):
    return lax.dot_general(left, right, (((1,), (1,)), ((), ())), preferred_element_type=F32)


def plain_dot(left, right):
    return jnp.dot(left, right, preferred_element_type=F32)


def row_blocks(rows):
    size = 256 if rows % 256 == 0 else rows
    return [(at, size) for at in range(0, rows, size)]


def masked_scores(lens, q, k, start):
    scores = right_dot(q, k) * (HEAD_DIM ** (-0.5))
    first = lens[0, 0]
    total = first + lens[0, 1]
    q_at = start + lax.broadcasted_iota(jnp.int32, (q.shape[0], 1), 0)
    k_at = lax.broadcasted_iota(jnp.int32, (1, k.shape[0]), 1)
    low = jnp.where(q_at >= total, total, jnp.where(q_at >= first, first, 0))
    seen = (k_at <= q_at) & (k_at >= low)
    return jnp.where(seen, scores, -1e30)


def softmax_parts(scores):
    peak = jnp.max(scores, axis=-1, keepdims=True)
    weights = jnp.exp(scores - peak)
    return weights / jnp.sum(weights, axis=-1, keepdims=True)


def attend_kernel(lens, q, k, v, out):
    for at, size in row_blocks(q.shape[0]):
        end = at + size
        probs = softmax_parts(masked_scores(lens, q[at:end, :], k[:end, :], at))
        out[at:end, :] = plain_dot(probs.astype(BF16), v[:end, :]).astype(BF16)


def attend_back_kernel(lens, q, k, v, d_att, d_q, d_k, d_v, k_sum, v_sum):
    scale = HEAD_DIM ** (-0.5)
    k_sum[...] = jnp.zeros_like(k_sum)
    v_sum[...] = jnp.zeros_like(v_sum)
    for at, size in row_blocks(q.shape[0]):
        end = at + size
        probs = softmax_parts(masked_scores(lens, q[at:end, :], k[:end, :], at))
        d_probs = right_dot(d_att[at:end, :], v[:end, :])
        v_sum[:end, :] += left_dot(probs.astype(BF16), d_att[at:end, :])
        inner = jnp.sum(probs * d_probs, axis=-1, keepdims=True)
        d_scores = (probs * (d_probs - inner)).astype(BF16)
        d_q[at:end, :] = (plain_dot(d_scores, k[:end, :]) * scale).astype(BF16)
        k_sum[:end, :] += left_dot(d_scores, q[at:end, :])
    d_k[...] = (k_sum[...] * scale).astype(BF16)
    d_v[...] = v_sum[...].astype(BF16)


def per_head(kernel, n_out, scratch, lens, *arrays):
    rows, width = arrays[0].shape
    spec = pl.BlockSpec((rows, HEAD_DIM), lambda h: (0, h))
    shape = jax.ShapeDtypeStruct((rows, width), BF16)
    return pl.pallas_call(
        kernel,
        grid=(width // HEAD_DIM,),
        in_specs=[pl.BlockSpec(memory_space=pltpu.SMEM)] + [spec] * len(arrays),
        out_specs=[spec] * n_out,
        out_shape=[shape] * n_out,
        scratch_shapes=[pltpu.VMEM((rows, HEAD_DIM), F32)] * scratch,
        compiler_params=pltpu.CompilerParams(vmem_limit_bytes=40 << 20),
        name=kernel.__name__,
    )(lens, *arrays)


class Plane:
    def __init__(self):
        self.me = lax.axis_index("tensor")

    def enter(self):
        barrier = pltpu.get_barrier_semaphore()
        for bit in range(2):
            pl.semaphore_signal(
                barrier, inc=1, device_id={"tensor": self.partner(bit)}, device_id_type=MESH
            )
        pl.semaphore_wait(barrier, 2)

    def mine(self, bit):
        return (self.me // (1 + bit)) % 2

    def partner(self, bit):
        return self.me + (1 - 2 * self.mine(bit)) * (1 + bit)

    def bit(self, chunk, step):
        return (chunk + step) % 2

    def place(self, chunk):
        return 2 * self.mine(self.bit(chunk, 0)) + self.mine(self.bit(chunk, 1))

    def scatter_copy(self, part, recv, send_sem, recv_sem, chunk, step):
        bit = self.bit(chunk, step)
        count = 2 - step
        held = 2 * self.mine(self.bit(chunk, 0)) if step else 0
        src = part.at[chunk, pl.ds(held + (1 - self.mine(bit)) * count, count)]
        return pltpu.make_async_remote_copy(
            src,
            recv[step].at[chunk],
            send_sem.at[chunk, step],
            recv_sem.at[chunk, step],
            device_id={"tensor": self.partner(bit)},
            device_id_type=MESH,
        )

    def gather_copy(self, whole, send_sem, recv_sem, chunk, step):
        bit = self.bit(chunk, step)
        count = 2 - step
        held = self.place(chunk) if step else 2 * self.mine(bit)
        ref = whole.at[chunk, pl.ds(held, count)]
        return pltpu.make_async_remote_copy(
            ref,
            ref,
            send_sem.at[chunk, step],
            recv_sem.at[chunk, step],
            device_id={"tensor": self.partner(bit)},
            device_id_type=MESH,
        )

    def halve(self, part, recv, send_sem, recv_sem, chunk):
        self.scatter_copy(part, recv, send_sem, recv_sem, chunk, 0).wait_recv()
        held = 2 * self.mine(self.bit(chunk, 0))
        for piece in range(2):
            part[chunk, held + piece] += recv[0][chunk, piece]
        self.scatter_copy(part, recv, send_sem, recv_sem, chunk, 1).start()

    def total(self, part, recv, send_sem, recv_sem, chunk):
        self.scatter_copy(part, recv, send_sem, recv_sem, chunk, 1).wait_recv()
        return part[chunk, self.place(chunk)] + recv[1][chunk, 0]


def own_pieces(array, chunks):
    rows, width = array.shape
    me = lax.axis_index("tensor")
    low, high = me % 2, me // 2
    pieces = array.reshape(chunks // 2, 2, 4, rows // chunks // 4, width)
    even = lax.dynamic_index_in_dim(pieces[:, 0], 2 * low + high, 1, keepdims=False)
    odd = lax.dynamic_index_in_dim(pieces[:, 1], 2 * high + low, 1, keepdims=False)
    return jnp.stack([even, odd], axis=1).reshape(chunks, -1, width).astype(F32)


def tiles(width, size):
    return [(at, min(at + size, width)) for at in range(0, width, size)]


def column_tiles(width):
    return tiles(width, 512)


def ffn_kernel(
    chunks,
    att_h, x_own_h, d_low_h, gain_h, w_out_h, w_gate_h, w_up_h, w_down_h,
    ffn_in_h, act_h, dg_h, du_h, d_res_h, resid_h, gain_grad_h,
    att, x_own, d_low, gain, w_out, w_gate, w_up, w_down,
    ffn_in, act, dg, du, gain_grad, scale,
    part, whole, recv0, recv1, send_sem, recv_sem, load_sem, store_sem, piece_sem,
):
    plane = Plane()
    recv = (recv0, recv1)
    rows = chunks * part.shape[1] * part.shape[2]
    size = rows // chunks
    width = part.shape[3]
    hidden = act.shape[1]
    loads = [
        pltpu.make_async_copy(src, dst, load_sem.at[i])
        for i, (src, dst) in enumerate(
            [
                (att_h, att), (w_out_h, w_out), (x_own_h, x_own), (gain_h, gain),
                (w_gate_h, w_gate), (w_up_h, w_up), (w_down_h, w_down), (d_low_h, d_low),
            ]
        )
    ]
    for load in loads:
        load.start()
    gain_grad[...] = jnp.zeros_like(gain_grad)
    plane.enter()
    loads[0].wait()
    loads[1].wait()

    def rows_of(c):
        return pl.ds(pl.multiple_of(c * size, size), size)

    def scatter(phase, c, step):
        return plane.scatter_copy(part, recv, send_sem.at[phase], recv_sem.at[phase], c, step)

    def gather(phase, ref, c, step):
        return plane.gather_copy(ref, send_sem.at[phase], recv_sem.at[phase], c, step)

    @pl.loop(0, chunks)
    def _(c):
        left = att[rows_of(c), :]
        for a, b in column_tiles(width):
            part[c, :, :, a:b] = plain_dot(left, w_out[:, a:b]).reshape(4, size // 4, b - a)
        scatter(0, c, 0).start()

    loads[2].wait()
    loads[3].wait()

    @pl.loop(0, chunks)
    def _(c):
        plane.halve(part, recv, send_sem.at[0], recv_sem.at[0], c)

    @pl.loop(0, chunks)
    def _(c):
        resid = x_own[c] + plane.total(part, recv, send_sem.at[0], recv_sem.at[0], c)
        x_own[c] = resid
        scale[c] = norm_scale(resid)
        whole[c, plane.place(c)] = resid * scale[c]
        gather(1, whole, c, 1).start()

    @pl.loop(0, chunks)
    def _(c):
        gather(1, whole, c, 1).wait_recv()
        gather(1, whole, c, 0).start()

    for load in loads[4:]:
        load.wait()
    store_resid = pltpu.make_async_copy(x_own, resid_h, store_sem.at[0])
    store_resid.start()

    @pl.loop(0, chunks)
    def _(c):
        gather(1, whole, c, 0).wait_recv()
        for piece in range(4):
            at = pl.ds(pl.multiple_of(c * size + piece * (size // 4), size // 4), size // 4)
            ffn_in[at, :] = (whole[c, piece] * gain[...]).astype(BF16)
        left = ffn_in[rows_of(c), :]
        for a, b in column_tiles(hidden):
            gate = plain_dot(left, w_gate[:, a:b])
            up = plain_dot(left, w_up[:, a:b])
            d_act = right_dot(d_low[rows_of(c), :], w_down[a:b, :])
            sigma = jax.nn.sigmoid(gate)
            act[rows_of(c), a:b] = (gate * sigma * up).astype(BF16)
            dg[rows_of(c), a:b] = (d_act * up * sigma * (1.0 + gate * (1.0 - sigma))).astype(BF16)
            du[rows_of(c), a:b] = (d_act * gate * sigma).astype(BF16)
        for step in range(2):
            scatter(0, c, step).wait_send()
        for a, b in column_tiles(width):
            sums = right_dot(dg[rows_of(c), :], w_gate[a:b, :]) + right_dot(du[rows_of(c), :], w_up[a:b, :])
            part[c, :, :, a:b] = sums.reshape(4, size // 4, b - a)
        scatter(2, c, 0).start()

    stores = [
        pltpu.make_async_copy(src, dst, store_sem.at[1 + i])
        for i, (src, dst) in enumerate([(ffn_in, ffn_in_h), (act, act_h), (dg, dg_h), (du, du_h)])
    ]
    for store in stores:
        store.start()

    @pl.loop(0, chunks)
    def _(c):
        plane.halve(part, recv, send_sem.at[2], recv_sem.at[2], c)

    @pl.loop(0, chunks)
    def _(c):
        d_in = plane.total(part, recv, send_sem.at[2], recv_sem.at[2], c)
        unit = whole[c, plane.place(c)]
        gain_grad[...] += jnp.sum(d_in * unit, axis=0, keepdims=True)
        d_unit = d_in * gain[...]
        mean = jnp.mean(d_unit * unit, axis=-1, keepdims=True)
        part[c, plane.place(c)] = scale[c] * (d_unit - unit * mean)
        piece = pltpu.make_async_copy(
            part.at[c, plane.place(c)], d_res_h.at[c, plane.place(c)], piece_sem
        )
        piece.start()
        piece.wait()
        gather(3, d_res_h, c, 1).start()

    store_gain = pltpu.make_async_copy(gain_grad, gain_grad_h, store_sem.at[5])
    store_gain.start()

    @pl.loop(0, chunks)
    def _(c):
        gather(3, d_res_h, c, 1).wait_recv()
        gather(3, d_res_h, c, 0).start()

    @pl.loop(0, chunks)
    def _(c):
        gather(3, d_res_h, c, 0).wait_recv()
        for step in range(2):
            gather(1, whole, c, step).wait_send()
            scatter(2, c, step).wait_send()
            gather(3, d_res_h, c, step).wait_send()

    store_resid.wait()
    store_gain.wait()
    for store in stores:
        store.wait()


def ffn_call(chunks, att, x_own, d_low, gain, w_out, w_gate, w_up, w_down):
    rows, inner = att.shape
    width = w_out.shape[1]
    hidden = w_gate.shape[1]
    piece = rows // chunks // 4
    out = jax.ShapeDtypeStruct
    pieces = (chunks, 4, piece, width)
    return pl.pallas_call(
        functools.partial(ffn_kernel, chunks),
        in_specs=[ANY] * 8,
        out_specs=[ANY] * 7,
        out_shape=[
            out((rows, width), BF16),
            out((rows, hidden), BF16),
            out((rows, hidden), BF16),
            out((rows, hidden), BF16),
            out(pieces, F32),
            out((chunks, piece, width), F32),
            out((1, width), F32),
        ],
        scratch_shapes=[
            pltpu.VMEM((rows, inner), BF16),
            pltpu.VMEM((chunks, piece, width), F32),
            pltpu.VMEM((rows, width), BF16),
            pltpu.VMEM((1, width), F32),
            pltpu.VMEM((inner, width), BF16),
            pltpu.VMEM((width, hidden), BF16),
            pltpu.VMEM((width, hidden), BF16),
            pltpu.VMEM((hidden, width), BF16),
            pltpu.VMEM((rows, width), BF16),
            pltpu.VMEM((rows, hidden), BF16),
            pltpu.VMEM((rows, hidden), BF16),
            pltpu.VMEM((rows, hidden), BF16),
            pltpu.VMEM((1, width), F32),
            pltpu.VMEM((chunks, piece, 1), F32),
            pltpu.VMEM(pieces, F32),
            pltpu.VMEM(pieces, F32),
            pltpu.VMEM((chunks, 2, piece, width), F32),
            pltpu.VMEM((chunks, 1, piece, width), F32),
            pltpu.SemaphoreType.DMA((4, chunks, 2)),
            pltpu.SemaphoreType.DMA((4, chunks, 2)),
            pltpu.SemaphoreType.DMA((8,)),
            pltpu.SemaphoreType.DMA((6,)),
            pltpu.SemaphoreType.DMA,
        ],
        compiler_params=pltpu.CompilerParams(
            collective_id=0, has_side_effects=True, vmem_limit_bytes=63 << 20
        ),
        name="ffn",
    )(att, x_own, d_low, gain, w_out, w_gate, w_up, w_down)


def last_kernel(
    chunks,
    act_h, w_down_h, resid_h, dq_h, dk_h, dv_h, w_q_h, w_k_h, w_v_h, x_own_h, kv_own_h, gain_x_h, gain_kv_h,
    out_h, d_x_h, d_kv_h, gain_grad_h,
    act, w_down, resid, dq, dk, dv, w_q, w_k, w_v, x_own, kv_own, gain_x, gain_kv,
    gain_grad, part_a, part_b, part_c, recv_a0, recv_a1, recv_b0, recv_b1, recv_c0, recv_c1,
    send_sem, recv_sem, load_sem, store_sem, piece_sem,
):
    plane = Plane()
    size = part_a.shape[1] * part_a.shape[2]
    width = part_a.shape[3]
    loads = [
        pltpu.make_async_copy(src, dst, load_sem.at[i])
        for i, (src, dst) in enumerate(
            [
                (act_h, act), (w_down_h, w_down), (dq_h, dq), (w_q_h, w_q), (dk_h, dk), (dv_h, dv), (w_k_h, w_k),
                (w_v_h, w_v), (resid_h, resid), (x_own_h, x_own), (kv_own_h, kv_own), (gain_x_h, gain_x),
                (gain_kv_h, gain_kv),
            ]
        )
    ]
    for load in loads:
        load.start()
    gain_grad[...] = jnp.zeros_like(gain_grad)
    plane.enter()

    def rows_of(c):
        return pl.ds(pl.multiple_of(c * size, size), size)

    sets = ((part_a, (recv_a0, recv_a1), out_h), (part_b, (recv_b0, recv_b1), d_x_h), (part_c, (recv_c0, recv_c1), d_kv_h))

    def scatter(which, c, step):
        part, recv, _ = sets[which]
        return plane.scatter_copy(part, recv, send_sem.at[which], recv_sem.at[which], c, step)

    def gather(which, c, step):
        return plane.gather_copy(sets[which][2], send_sem.at[3 + which], recv_sem.at[3 + which], c, step)

    for load in loads[:2]:
        load.wait()

    @pl.loop(0, chunks)
    def _(c):
        for a, b in column_tiles(width):
            sums = plain_dot(act[rows_of(c), :], w_down[:, a:b])
            part_a[c, :, :, a:b] = sums.reshape(4, size // 4, b - a)
        scatter(0, c, 0).start()

    for load in loads[2:4]:
        load.wait()

    @pl.loop(0, chunks)
    def _(c):
        for a, b in column_tiles(width):
            sums = right_dot(dq[rows_of(c), :], w_q[a:b, :])
            part_b[c, :, :, a:b] = sums.reshape(4, size // 4, b - a)
        scatter(1, c, 0).start()

    for load in loads[4:8]:
        load.wait()

    @pl.loop(0, chunks)
    def _(c):
        for a, b in column_tiles(width):
            sums = right_dot(dk[rows_of(c), :], w_k[a:b, :]) + right_dot(dv[rows_of(c), :], w_v[a:b, :])
            part_c[c, :, :, a:b] = sums.reshape(4, size // 4, b - a)
        scatter(2, c, 0).start()

    for load in loads[8:]:
        load.wait()

    def finish(which, c):
        part, recv, whole = sets[which]
        got = plane.total(part, recv, send_sem.at[which], recv_sem.at[which], c)
        if which == 0:
            part[c, plane.place(c)] = resid[c] + got
        else:
            own, gain = ((x_own, gain_x), (kv_own, gain_kv))[which - 1]
            scale = norm_scale(own[c])
            unit = own[c] * scale
            gain_grad[which - 1] += jnp.sum(got * unit, axis=0, keepdims=True)
            d_unit = got * gain[...]
            mean = jnp.mean(d_unit * unit, axis=-1, keepdims=True)
            part[c, plane.place(c)] = scale * (d_unit - unit * mean)
        piece = pltpu.make_async_copy(part.at[c, plane.place(c)], whole.at[c, plane.place(c)], piece_sem)
        piece.start()
        piece.wait()
        gather(which, c, 1).start()

    for which in range(3):
        part, recv, _ = sets[which]

        @pl.loop(0, chunks)
        def _(c):
            plane.halve(part, recv, send_sem.at[which], recv_sem.at[which], c)

    for which in range(3):

        @pl.loop(0, chunks)
        def _(c):
            finish(which, c)

    store_gain = pltpu.make_async_copy(gain_grad, gain_grad_h, store_sem)
    store_gain.start()

    for which in range(3):

        @pl.loop(0, chunks)
        def _(c):
            gather(which, c, 1).wait_recv()
            gather(which, c, 0).start()

    for which in range(3):

        @pl.loop(0, chunks)
        def _(c):
            gather(which, c, 0).wait_recv()
            for step in range(2):
                scatter(which, c, step).wait_send()
                gather(which, c, step).wait_send()

    store_gain.wait()


def last_call(chunks, act, w_down, resid, dq, dk, dv, w_q, w_k, w_v, x_own, kv_own, gain_x, gain_kv):
    rows, hidden = act.shape
    inner = dq.shape[1]
    width = w_down.shape[1]
    piece = rows // chunks // 4
    out = jax.ShapeDtypeStruct
    pieces = (chunks, 4, piece, width)
    own = pltpu.VMEM((chunks, piece, width), F32)
    return pl.pallas_call(
        functools.partial(last_kernel, chunks),
        in_specs=[ANY] * 13,
        out_specs=[ANY] * 4,
        out_shape=[out(pieces, F32), out(pieces, F32), out(pieces, F32), out((2, 1, width), F32)],
        scratch_shapes=[
            pltpu.VMEM((rows, hidden), BF16),
            pltpu.VMEM((hidden, width), BF16),
            own,
            pltpu.VMEM((rows, inner), BF16),
            pltpu.VMEM((rows, inner), BF16),
            pltpu.VMEM((rows, inner), BF16),
            pltpu.VMEM((width, inner), BF16),
            pltpu.VMEM((width, inner), BF16),
            pltpu.VMEM((width, inner), BF16),
            own,
            own,
            pltpu.VMEM((1, width), F32),
            pltpu.VMEM((1, width), F32),
            pltpu.VMEM((2, 1, width), F32),
            pltpu.VMEM(pieces, F32),
            pltpu.VMEM(pieces, F32),
            pltpu.VMEM(pieces, F32),
        ]
        + [pltpu.VMEM((chunks, 2, piece, width), F32), pltpu.VMEM((chunks, 1, piece, width), F32)] * 3
        + [
            pltpu.SemaphoreType.DMA((6, chunks, 2)),
            pltpu.SemaphoreType.DMA((6, chunks, 2)),
            pltpu.SemaphoreType.DMA((13,)),
            pltpu.SemaphoreType.DMA,
            pltpu.SemaphoreType.DMA,
        ],
        compiler_params=pltpu.CompilerParams(
            collective_id=1, has_side_effects=True, vmem_limit_bytes=63 << 20
        ),
        cost_estimate=pl.CostEstimate(flops=3 * 10**11, bytes_accessed=10**8, transcendentals=0),
        name="last",
    )(act, w_down, resid, dq, dk, dv, w_q, w_k, w_v, x_own, kv_own, gain_x, gain_kv)


CHUNKS = 4


def body(
    hidden, kv_input, attn_norm, w_query, w_key, w_value, w_out, kv_norm, ffn_norm, w_gate, w_up, w_down, seq_lengths, cotangent
):
    rows, width = hidden.shape
    total = seq_lengths[0, 0] + seq_lengths[0, 1]
    live = (jnp.arange(rows, dtype=jnp.int32) < total).astype(F32)[:, None]

    x_full = hidden.astype(F32)
    normed = (x_full * norm_scale(x_full) * attn_norm).astype(BF16)
    query = plain_dot(normed, w_query).astype(BF16)
    kv_full = kv_input.astype(F32)
    scale_kv = norm_scale(kv_full)
    kv_normed = (kv_full * scale_kv * kv_norm).astype(BF16)
    keys = plain_dot(kv_normed, w_key).astype(BF16)
    values = plain_dot(kv_normed, w_value).astype(BF16)
    (attended,) = per_head(attend_kernel, 1, 0, seq_lengths, query, keys, values)

    d_out = cotangent.astype(F32) * live
    d_out_low = d_out.astype(BF16)
    x_own = own_pieces(hidden, CHUNKS)
    kv_own = own_pieces(kv_input, CHUNKS)
    ffn_in, activated, d_gate, d_up, d_res, resid_own, grad_ffn_norm = ffn_call(
        CHUNKS, attended, x_own, d_out_low, ffn_norm[None], w_out, w_gate, w_up, w_down
    )

    g_gate, g_up, g_down = left_dot(ffn_in, d_gate), left_dot(ffn_in, d_up), left_dot(activated, d_out_low)
    g_gate, g_up, g_down, d_res = lax.optimization_barrier((g_gate, g_up, g_down, d_res))
    grad_gate = lax.psum_scatter(g_gate, "dp", scatter_dimension=0, tiled=True)
    grad_up = lax.psum_scatter(g_up, "dp", scatter_dimension=0, tiled=True)
    grad_down = lax.psum_scatter(g_down, "dp", scatter_dimension=1, tiled=True)

    d_resid = d_out + d_res.reshape(rows, width)
    d_branch = d_resid.astype(BF16)
    grad_out = lax.psum_scatter(left_dot(attended, d_branch), "dp", scatter_dimension=1, tiled=True)
    d_att = right_dot(d_branch, w_out).astype(BF16)
    d_query, d_keys, d_values = per_head(attend_back_kernel, 3, 2, seq_lengths, query, keys, values, d_att)
    g_query, g_key, g_value = left_dot(normed, d_query), left_dot(kv_normed, d_keys), left_dot(kv_normed, d_values)
    g_query, g_key, g_value, d_query = lax.optimization_barrier((g_query, g_key, g_value, d_query))
    grad_query = lax.psum_scatter(g_query, "dp", scatter_dimension=0, tiled=True)
    grad_key = lax.psum_scatter(g_key, "dp", scatter_dimension=0, tiled=True)
    grad_value = lax.psum_scatter(g_value, "dp", scatter_dimension=0, tiled=True)

    summed, d_x, d_kv, grad_norms = last_call(
        CHUNKS, activated, w_down, resid_own, d_query, d_keys, d_values, w_query, w_key, w_value, x_own, kv_own,
        attn_norm[None], kv_norm[None],
    )
    output = (summed.reshape(rows, width) * live).astype(BF16)
    grad_input = (d_resid + d_x.reshape(rows, width)).astype(BF16)
    grad_kv_input = d_kv.reshape(rows, width).astype(BF16)

    gains = jnp.stack([grad_norms[0, 0], grad_norms[1, 0], grad_ffn_norm[0]])
    gains = lax.psum_scatter(lax.psum(gains, "tensor"), "dp", scatter_dimension=1, tiled=True)
    return (
        output, grad_input, grad_kv_input, gains[0], grad_query, grad_key, grad_value, grad_out, gains[1], gains[2],
        grad_gate, grad_up, grad_down,
    )


def norm_back(d_normed, unit, scale_row, gain):
    gain_grad = jnp.sum(d_normed * unit, axis=0)
    d_unit = d_normed * gain
    d_in = scale_row * (d_unit - unit * jnp.mean(d_unit * unit, axis=-1, keepdims=True))
    return (gain_grad, d_in)


def plain_body(
    hidden,
    kv_input,
    attn_norm,
    w_query,
    w_key,
    w_value,
    w_out,
    kv_norm,
    ffn_norm,
    w_gate,
    w_up,
    w_down,
    seq_lengths,
    cotangent,
):
    rows = hidden.shape[0]
    width = w_query.shape[1]
    heads = width // HEAD_DIM
    scale = HEAD_DIM ** (-0.5)
    first = seq_lengths[0, 0]
    total = first + seq_lengths[0, 1]
    places = jnp.arange(rows, dtype=jnp.int32)
    segment = (places >= first).astype(jnp.int32) + (places >= total).astype(jnp.int32)
    allowed = (segment[:, None] == segment[None, :]) & (places[None, :] <= places[:, None])
    live = (places < total).astype(F32)[:, None]
    x_full = hidden.astype(F32)
    scale_attn = norm_scale(x_full)
    unit_attn = x_full * scale_attn
    normed = (unit_attn * attn_norm).astype(BF16)
    query = jnp.dot(normed, w_query, preferred_element_type=F32).astype(BF16)
    kv_full = kv_input.astype(F32)
    scale_kv = norm_scale(kv_full)
    unit_kv = kv_full * scale_kv
    kv_normed = (unit_kv * kv_norm).astype(BF16)
    keys = jnp.dot(kv_normed, w_key, preferred_element_type=F32).astype(BF16)
    values = jnp.dot(kv_normed, w_value, preferred_element_type=F32).astype(BF16)
    q_heads = query.reshape(rows, heads, HEAD_DIM)
    k_heads = keys.reshape(rows, heads, HEAD_DIM)
    v_heads = values.reshape(rows, heads, HEAD_DIM)

    def scores_of():
        raw = (
            jnp.einsum("qhd,khd->hqk", q_heads, k_heads, preferred_element_type=F32) * scale
        )
        return jnp.where(allowed[None], raw, -1e30)

    scores = scores_of()
    peak = jnp.max(scores, axis=-1, keepdims=True)
    weights = jnp.exp(scores - peak)
    row_total = jnp.sum(weights, axis=-1, keepdims=True)
    log_total = peak + jnp.log(row_total)
    probs_low = (weights / row_total).astype(BF16)
    attended = jnp.einsum("hqk,khd->qhd", probs_low, v_heads, preferred_element_type=F32)
    attended = attended.astype(BF16).reshape(rows, width)
    branch = lax.psum(jnp.dot(attended, w_out, preferred_element_type=F32), "tensor")
    resid = x_full + branch
    scale_ffn = norm_scale(resid)
    unit_ffn = resid * scale_ffn
    ffn_in = (unit_ffn * ffn_norm).astype(BF16)
    gate_pre, up_pre = (
        jnp.dot(ffn_in, w_gate, preferred_element_type=F32),
        jnp.dot(ffn_in, w_up, preferred_element_type=F32),
    )
    activated = (jax.nn.silu(gate_pre) * up_pre).astype(BF16)
    ffn_out = lax.psum(jnp.dot(activated, w_down, preferred_element_type=F32), "tensor")
    output = ((resid + ffn_out) * live).astype(BF16)
    d_out = cotangent.astype(F32) * live
    d_out_low = d_out.astype(BF16)
    grad_down = left_dot(activated, d_out_low)
    d_act = right_dot(d_out_low, w_down)
    gate_use, up_use = (gate_pre, up_pre)
    sigma = jax.nn.sigmoid(gate_use)
    d_gate = (d_act * up_use * sigma * (1.0 + gate_use * (1.0 - sigma))).astype(BF16)
    d_up = (d_act * gate_use * sigma).astype(BF16)
    grad_gate = left_dot(ffn_in, d_gate)
    grad_up = left_dot(ffn_in, d_up)
    d_ffn_in = lax.psum(right_dot(d_gate, w_gate) + right_dot(d_up, w_up), "tensor")
    grad_ffn_norm, d_res_norm = norm_back(d_ffn_in, unit_ffn, scale_ffn, ffn_norm)
    d_resid = d_out + d_res_norm
    d_branch = d_resid.astype(BF16)
    grad_out = left_dot(attended, d_branch)
    d_att = right_dot(d_branch, w_out).astype(BF16).reshape(rows, heads, HEAD_DIM)
    probs = jnp.exp(scores_of() - log_total)
    probs_back = probs.astype(BF16)
    d_probs = jnp.einsum("qhd,khd->hqk", d_att, v_heads, preferred_element_type=F32)
    d_values = jnp.einsum("hqk,qhd->khd", probs_back, d_att, preferred_element_type=F32)
    d_values = d_values.astype(BF16).reshape(rows, width)
    inner = jnp.sum(probs * d_probs, axis=-1, keepdims=True)
    d_scores = (probs * (d_probs - inner)).astype(BF16)
    d_query = (
        jnp.einsum("hqk,khd->qhd", d_scores, k_heads, preferred_element_type=F32) * scale
    )
    d_query = d_query.astype(BF16).reshape(rows, width)
    d_keys = (
        jnp.einsum("hqk,qhd->khd", d_scores, q_heads, preferred_element_type=F32) * scale
    )
    d_keys = d_keys.astype(BF16).reshape(rows, width)
    grad_query = left_dot(normed, d_query)
    grad_key = left_dot(kv_normed, d_keys)
    grad_value = left_dot(kv_normed, d_values)
    d_normed, d_kv_normed = lax.psum(
        (right_dot(d_query, w_query), right_dot(d_keys, w_key) + right_dot(d_values, w_value)),
        "tensor",
    )
    grad_attn_norm, d_x = norm_back(d_normed, unit_attn, scale_attn, attn_norm)
    grad_kv_norm, d_kv = norm_back(d_kv_normed, unit_kv, scale_kv, kv_norm)
    grad_input = (d_resid + d_x).astype(BF16)
    grad_kv_input = d_kv.astype(BF16)
    parts = (
        lax.psum_scatter(grad_attn_norm, "dp", scatter_dimension=0, tiled=True),
        lax.psum_scatter(grad_query, "dp", scatter_dimension=0, tiled=True),
        lax.psum_scatter(grad_key, "dp", scatter_dimension=0, tiled=True),
        lax.psum_scatter(grad_value, "dp", scatter_dimension=0, tiled=True),
        lax.psum_scatter(grad_out, "dp", scatter_dimension=1, tiled=True),
        lax.psum_scatter(grad_kv_norm, "dp", scatter_dimension=0, tiled=True),
        lax.psum_scatter(grad_ffn_norm, "dp", scatter_dimension=0, tiled=True),
        lax.psum_scatter(grad_gate, "dp", scatter_dimension=0, tiled=True),
        lax.psum_scatter(grad_up, "dp", scatter_dimension=0, tiled=True),
        lax.psum_scatter(grad_down, "dp", scatter_dimension=1, tiled=True),
    )
    return (
        output,
        grad_input,
        grad_kv_input,
        parts[0],
        parts[1],
        parts[2],
        parts[3],
        parts[4],
        parts[5],
        parts[6],
        parts[7],
        parts[8],
        parts[9],
    )


def solution(mesh):
    in_specs = (
        P("dp", None), P("dp", None), P(), P(None, "tensor"), P(None, "tensor"), P(None, "tensor"), P("tensor", None),
        P(), P(), P(None, "tensor"), P(None, "tensor"), P("tensor", None), P("dp", None), P("dp", None),
    )
    out_specs = (
        P("dp", None), P("dp", None), P("dp", None), P("dp"), P("dp", "tensor"), P("dp", "tensor"), P("dp", "tensor"),
        P("tensor", "dp"), P("dp"), P("dp"), P("dp", "tensor"), P("dp", "tensor"), P("tensor", "dp"),
    )
    program = body if mesh.shape["tensor"] == 4 else plain_body
    return jax.shard_map(program, mesh=mesh, in_specs=in_specs, out_specs=out_specs, check_vma=False)
```

time: 1340 us -> 1250 us (0.933)
  Pallas kernels: 0 us -> 540 us
  waiting for transfers between devices: 1050 us -> 558 us
  matrix products: 154 us -> 62.9 us
  other arithmetic: 59.7 us -> 30.5 us
  blocking collectives: 30.7 us -> 9.89 us
  local copies, waits for them, and re-layouts: 11.6 us -> 27.4 us
    psum x3 -> x0, waiting for transfers between devices: 550 us -> none  [the longest x1 280 us: body(): lax.psum(jnp.dot(activated, w_down, preferred_element_type=jnp.float32),...]
    pallas_call x0 -> x4, Pallas kernels: none -> 540 us  [the longest x1 310 us: last_call(): pl.pallas_call(functools.partial(last_kernel, chunks), in_specs=[ANY] * 1...]
    dot_general x13 -> x3, matrix products: 55.1 us -> 7.27 us  [plain_dot(): return jnp.dot(left, right, preferred_element_type=F32)]
    reduce_scatter x7, waiting for transfers between devices: 503 us -> 547 us  [the longest x1 118 us: body(): grad_down = lax.psum_scatter(g_down, 'dp', scatter_dimension=1, tiled=True)]
    dot_general x7 -> x1, matrix products: 39.3 us -> 1.82 us  [right_dot(): lax.dot_general(left, right, (((1,), (1,)), ((), ())), preferred_element_...]
    unnamed x1 -> x0, blocking collectives: 30.7 us -> none
    reduce_sum x7 -> x2, other arithmetic: 25.3 us -> 3.4 us  [norm_scale(): return lax.rsqrt(jnp.mean(values * values, axis=-1, keepdims=True) + EPS)]
    convert_element_type x5 -> x7, other arithmetic: 28.5 us -> 26.9 us  [the longest x1 10.1 us: body(): grad_input = (d_resid + d_x.reshape(rows, width)).astype(BF16)]
  transfers between devices with their start and end apart: 10 -> 8, of which waited for: 9 -> 8; matrix products, arithmetic and copies ran while one was open for 7% -> 2% of each run, Pallas kernels for 0% -> 0%
where the time goes in v1:
time: 1250 us
  waiting for transfers between devices  558 us (45%)
  Pallas kernels  540 us (43%)
  matrix products  62.9 us (5%)
  other arithmetic  30.5 us (2%)
  local copies, waits for them, and re-layouts  27.4 us (2%)
  between operations  16.1 us (1%)
    pallas_call x1, Pallas kernels, last_call(): pl.pallas_call(functools.partial(last_kernel, chunks), in_specs=[ANY] * 1...  310 us
    pallas_call x1, Pallas kernels, ffn_call(): pl.pallas_call(functools.partial(ffn_kernel, chunks), in_specs=[ANY] * 8,...  212 us
    reduce_scatter x1, waiting for transfers between devices, body(): grad_down = lax.psum_scatter(g_down, 'dp', scatter_dimension=1, tiled=True)  118 us
    reduce_scatter x1, waiting for transfers between devices, body(): grad_up = lax.psum_scatter(g_up, 'dp', scatter_dimension=0, tiled=True)  118 us
    reduce_scatter x1, waiting for transfers between devices, body(): grad_gate = lax.psum_scatter(g_gate, 'dp', scatter_dimension=0, tiled=True)  118 us
    dot_general x7, matrix products, left_dot(): lax.dot_general(left, right, (((0,), (0,)), ((), ())), preferred_element_...  53.8 us
    reduce_scatter x1, waiting for transfers between devices, body(): lax.psum_scatter(g_query, 'dp', scatter_dimension=0, tiled=True)  51 us
    reduce_scatter x1, waiting for transfers between devices, body(): lax.psum_scatter(g_value, 'dp', scatter_dimension=0, tiled=True)  50.9 us
  transfers between devices with their start and end apart: 8, of which 8 were waited for; matrix products, arithmetic and copies ran while one was open for 2% of the time, Pallas kernels for 0%

profile of v1, /device:TPU:0, one launch (start us, length us, event | category | flops | bytes accessed | tf_op | source)
XLA Modules:
  0.0 1245.6 jit_solution(9172088961600620839)
XLA Ops:
  7.2 0.0 reduce-scatter.25.cloned.1.call-start
  7.3 1.4 fusion.23
  10.0 2.7 fusion
  12.8 0.7 fusion.3
  13.5 3.6 convolution_convert_fusion.1.v
  17.1 1.9 convolution_convert_fusion.2.k
  18.9 1.4 fusion.20
  20.4 1.2 dynamic-slice_bitcast_fusion
  21.6 0.1 pad_maximum_fusion.1
  21.7 1.4 bitcast_convert_fusion.kv_own_h
  23.0 0.3 fusion.21
  23.4 0.1 dynamic-slice_bitcast_fusion.2
  23.4 0.1 pad_maximum_fusion
  23.5 1.4 bitcast_convert_fusion.1.x_own_h
  24.9 8.5 copy.29.w_gate_h
  33.5 8.3 copy.30.w_up_h
  41.8 4.3 fusion.8.d_low_h
  46.1 1.8 convolution_convert_fusion.3.q
  47.9 7.3 attend_kernel.1.att_h
  55.2 0.9 copy-done
  56.1 212.3 %ffn.1 = (bf16[768,2048]{1,0:T(8,128)(2,1)}, bf16[768,1376]{1,0:T(8,128)(2,1)}, bf16[768,1376]{1,0:T(8,128)(2,1)}, bf16[768,1376]{1,0:T(8,128)(2,1)}, f32[4,4,48...) custom-call(bf16[768,512]{1,0:T(8,128)(2,1)} %copy-done, ...), custom_call_target="tpu_custom_call" | custom-call | tf_op jit(solution)/shard_map/ffn/pallas_call | solution.py:326
  268.4 11.4 fusion.26
  279.8 11.4 fusion.24
  291.2 9.6 fusion.25
  300.8 4.6 fusion.9
  305.5 1.8 convolution_convert_fusion.d_att
  307.4 0.6 copy-done.5
  308.0 11.2 attend_back_kernel.1
  319.3 0.8 copy-done.7
  320.1 4.0 fusion.10
  324.2 5.8 fusion.16
  330.0 5.8 fusion.14
  335.9 309.7 %last.1 = (f32[4,4,48,2048]{3,2,1,0:T(8,128)}, f32[4,4,48,2048]{3,2,1,0:T(8,128)}, f32[4,4,48,2048]{3,2,1,0:T(8,128)}, f32[2,1,2048]{2,1,0:T(1,128)}) custom-call(bf16[768,1376]{1,0:T(8,128)(2,1)} %get-tuple-element.35.act_h, bf16[1376,2048]{1,0:T(8,128)(2,1)} %w_down_h.3, f32[4,48,2048]{2,1,0:T(8,128)} %get-tuple-element.36.resid_h, ...), custom_call_target="tpu_custom_call" | custom-call | flops 299999985664 | bytes 100000000 | tf_op jit(solution)/shard_map/last/pallas_call | solution.py:503
  645.6 0.7 slice_bitcast_fusion.1
  646.3 1.3 copy.31
  647.6 0.0 reduce-scatter.25.cloned.1.call-update
  647.7 0.0 reduce-scatter.17.cloned.1.call-start
  647.7 5.7 fusion.27
  653.4 0.0 reduce-scatter.17.cloned.1.call-update
  653.4 0.0 reduce-scatter.11.cloned.1.call-start
  653.5 0.7 reduce-scatter.11.cloned.1.call-update
  654.2 0.0 reduce-scatter.13.cloned.1.call-start
  654.2 0.5 reduce-scatter.13.cloned.1.call-update
  654.8 0.0 reduce-scatter.15.cloned.1.call-start
  654.8 0.5 reduce-scatter.15.cloned.1.call-update
  655.3 0.0 reduce-scatter.19.cloned.1.call-start
  655.4 0.5 reduce-scatter.19.cloned.1.call-update
  655.9 0.0 reduce-scatter.21.cloned.1.call-start
  656.0 0.7 reduce-scatter.21.cloned.1.call-update
  656.7 0.0 reduce-scatter.23.cloned.1.call-start
  656.7 0.7 reduce-scatter.23.cloned.1.call-update
  657.4 5.1 convert_element_type.80
  662.6 10.1 fusion.6
  672.7 7.8 reduce-scatter.25.cloned.1.call-done
  680.5 1.0 copy.32
  681.5 9.9 psum.8
  691.4 0.6 fusion.22
  692.0 39.7 %reduce-scatter.17.cloned.1.call-done = f32[512,256]{1,0:T(8,128)} async-done(((f32[512,2048]{1,0:T(8,128)}), f32[512,256]{1,0:T(8,128)}) %reduce-scatter.17.cloned.1.call-update) | async-done | bytes 524304 | tf_op jit(solution)/shard_map/reduce_scatter | solution.py:579
  731.7 51.0 %reduce-scatter.11.cloned.1.call-done = f32[256,512]{1,0:T(8,128)} async-done(((f32[2048,512]{1,0:T(8,128)}), f32[256,512]{1,0:T(8,128)}) %reduce-scatter.11.cloned.1.call-update) | async-done | bytes 524304 | tf_op jit(solution)/shard_map/reduce_scatter | solution.py:584
  782.7 50.9 %reduce-scatter.13.cloned.1.call-done = f32[256,512]{1,0:T(8,128)} async-done(((f32[2048,512]{1,0:T(8,128)}), f32[256,512]{1,0:T(8,128)}) %reduce-scatter.13.cloned.1.call-update) | async-done | bytes 524304 | tf_op jit(solution)/shard_map/reduce_scatter | solution.py:585
  833.6 50.9 %reduce-scatter.15.cloned.1.call-done = f32[256,512]{1,0:T(8,128)} async-done(((f32[2048,512]{1,0:T(8,128)}), f32[256,512]{1,0:T(8,128)}) %reduce-scatter.15.cloned.1.call-update) | async-done | bytes 524304 | tf_op jit(solution)/shard_map/reduce_scatter | solution.py:586
  884.5 117.8 %reduce-scatter.19.cloned.1.call-done = f32[256,1376]{0,1:T(8,128)} async-done(((f32[2048,1376]{0,1:T(8,128)}), f32[256,1376]{0,1:T(8,128)}) %reduce-scatter.19.cloned.1.call-update) | async-done | bytes 1409040 | tf_op jit(solution)/shard_map/reduce_scatter | solution.py:573
  1002.3 118.1 %reduce-scatter.21.cloned.1.call-done = f32[256,1376]{0,1:T(8,128)} async-done(((f32[2048,1376]{0,1:T(8,128)}), f32[256,1376]{0,1:T(8,128)}) %reduce-scatter.21.cloned.1.call-update) | async-done | bytes 1409040 | tf_op jit(solution)/shard_map/reduce_scatter | solution.py:574
  1120.4 118.1 %reduce-scatter.23.cloned.1.call-done = f32[1376,256]{1,0:T(8,128)} async-done(((f32[1376,2048]{1,0:T(8,128)}), f32[1376,256]{1,0:T(8,128)}) %reduce-scatter.23.cloned.1.call-update) | async-done | bytes 1409040 | tf_op jit(solution)/shard_map/reduce_scatter | solution.py:575
  (53 shorter events, 0.2 us)
Async XLA Ops:
  7.2 5.6 copy-start.15
  7.2 673.3 %reduce-scatter.25.cloned.1.call-start = ((), (), s32[]{:S(2)}) async-start(), calls=%async_computation.15 | async-start | bytes 1179648
  10.0 290.8 %copy-start.18 = (f32[768]{0:T(1024)}, f32[768]{0:T(1024)S(1)}, u32[]{:S(2)}) copy-start(f32[768]{0:T(1024)S(1)} %fusion.13) | copy-start | bytes 9220
  10.0 3.5 copy-start.16
  10.0 3.5 copy-start.25
  13.5 3.6 copy-start.23
  18.9 29.0 %copy-start.2 = (bf16[768,512]{1,0:T(8,128)(2,1)}, bf16[768,512]{1,0:T(8,128)(2,1)S(1)}, u32[]{:S(2)}) copy-start(bf16[768,512]{1,0:T(8,128)(2,1)S(1)} %convolution_convert_fusion.2.k) | copy-start | bytes 2359300
  20.4 2.7 copy-start.12
  41.7 4.3 copy-start.13
  41.8 4.3 copy-start.22
  41.8 4.3 copy-start.24
  46.0 1.9 copy-start.6
  47.9 7.3 copy-start.4
  55.2 0.9 copy-start
  279.8 11.4 copy-start.21
  300.8 4.7 copy-start.17
  305.5 1.9 copy-start.11
  305.5 1.9 copy-start.3
  305.5 2.5 copy-start.5
  308.0 12.1 copy-start.14
  319.2 0.9 copy-start.7
  319.3 4.9 copy-start.8
  319.3 10.7 copy-start.9
  335.9 310.4 %copy-start.20 = (f32[1,2048]{1,0:T(1,128)S(1)}, f32[1,2048]{1,0:T(1,128)}, u32[]{:S(2)}) copy-start(f32[1,2048]{1,0:T(1,128)} %get-tuple-element.50) | copy-start | bytes 24580
  335.9 311.9 %copy-start.1 = (bf16[768,512]{1,0:T(8,128)(2,1)S(1)}, bf16[768,512]{1,0:T(8,128)(2,1)}, u32[]{:S(2)}) copy-start(bf16[768,512]{1,0:T(8,128)(2,1)} %copy-done) | copy-start | bytes 2359300
  647.7 84.0 %reduce-scatter.17.cloned.1.call-start = ((), (), s32[]{:S(2)}) async-start(), calls=%async_computation.11 | async-start | bytes 4718592 | tf_op jit(solution)/shard_map/reduce_scatter | solution.py:579
  653.4 129.3 %reduce-scatter.11.cloned.1.call-start = ((), (), s32[]{:S(2)}) async-start(), calls=%async_computation.8 | async-start | bytes 4718592 | tf_op jit(solution)/shard_map/reduce_scatter | solution.py:584
  654.2 179.4 %reduce-scatter.13.cloned.1.call-start = ((), (), s32[]{:S(2)}) async-start(), calls=%async_computation.9 | async-start | bytes 4718592 | tf_op jit(solution)/shard_map/reduce_scatter | solution.py:585
  654.8 229.8 %reduce-scatter.15.cloned.1.call-start = ((), (), s32[]{:S(2)}) async-start(), calls=%async_computation.10 | async-start | bytes 4718592 | tf_op jit(solution)/shard_map/reduce_scatter | solution.py:586
  655.3 347.0 %reduce-scatter.19.cloned.1.call-start = ((), (), s32[]{:S(2)}) async-start(), calls=%async_computation.12 | async-start | bytes 12681216 | tf_op jit(solution)/shard_map/reduce_scatter | solution.py:573
  655.9 464.5 %reduce-scatter.21.cloned.1.call-start = ((), (), s32[]{:S(2)}) async-start(), calls=%async_computation.13 | async-start | bytes 12681216 | tf_op jit(solution)/shard_map/reduce_scatter | solution.py:574
  656.7 581.8 %reduce-scatter.23.cloned.1.call-start = ((), (), s32[]{:S(2)}) async-start(), calls=%async_computation.14 | async-start | bytes 12681216 | tf_op jit(solution)/shard_map/reduce_scatter | solution.py:575
  657.4 5.1 copy-start.10
  657.4 5.1 copy-start.19
Sparse Core Ops, SparseCore 0:
  647.8 32.6 reduce-scatter.24
  683.4 48.2 reduce-scatter.16
  734.6 48.1 reduce-scatter.10
  785.4 48.1 reduce-scatter.12
  836.3 48.1 reduce-scatter.14
  887.3 114.9 reduce-scatter.18
  1005.2 115.1 reduce-scatter.20
  1123.3 115.1 reduce-scatter.22
